TPU v7x, 32 devices: a whole 2x2x4 slice. The times are simulated.
32 devices in a mesh: outer: 4 (over x, core), dp: 4 (over z), mp: 2 (over y).
Axes of the slice: x: 2, y: 2, z: 4, core: 2. Of those that a mesh axis runs over, the one named last changes fastest.
Arguments:
- tokens: bfloat16 [4, 4096, 2048], P('outer', 'dp'), may hold values from -6 to 6
- cotangent: bfloat16 [4, 4096, 2048], P('outer', 'dp'), may hold values from -0.59765625 to 0.59765625
- gate_weight: bfloat16 [4, 2048, 6144], P('outer', 'dp', 'mp'), may hold values from -0.125 to 0.125
- up_weight: bfloat16 [4, 2048, 6144], P('outer', 'dp', 'mp'), may hold values from -0.125 to 0.125
- down_master: float32 [4, 6144, 2048], P('outer', 'mp', 'dp'), may hold values from -0.0375 to 0.0375
- first_moment: float32 [4, 6144, 2048], P('outer', 'mp', 'dp'), may hold values from -0.6 to 0.6
- second_moment: float32 [4, 6144, 2048], P('outer', 'mp', 'dp'), may hold values from 1 to 10
- anchor: float32 [6144, 2048], P('mp', 'dp'), may hold values from -0.0375 to 0.0375
- outer_momentum: float32 [6144, 2048], P('mp', 'dp'), may hold values from -0.00018 to 0.00018
Outputs:
- new_params: float32 [6144, 2048], P('mp', 'dp')
- first_out: float32 [4, 6144, 2048], P('outer', 'mp', 'dp')
- second_out: float32 [4, 6144, 2048], P('outer', 'mp', 'dp')
- momentum_out: float32 [6144, 2048], P('mp', 'dp')
- input_grad: bfloat16 [4, 4096, 2048], P('outer', ('dp', 'mp'))
All inputs are finite; a program needn't handle non-finite values.
Results may differ from a plain program's by a relative error of at most 0.023.
Values may be sent and summed in bfloat16 or wider, within the bound.
A program may use at most 256 MiB of HBM per device.

v0:
```python
import jax
import jax.numpy as jnp
from jax import lax
from jax.sharding import PartitionSpec as P

bias_one = 1.0 - (0.9**50) ** 2
bias_two = 1.0 - (0.999**50) ** 2


def shards(
    tokens,
    cotangent,
    gate_weight,
    up_weight,
    down_master,
    first_moment,
    second_moment,
    anchor,
    outer_momentum,
):
    inputs = tokens[0]
    upstream = cotangent[0]
    gate_full, up_full = (
        lax.all_gather(gate_weight[0], "dp", axis=0, tiled=True),
        lax.all_gather(up_weight[0], "dp", axis=0, tiled=True),
    )
    gate_pre = jnp.dot(inputs, gate_full, preferred_element_type=jnp.float32)
    up_pre = jnp.dot(inputs, up_full, preferred_element_type=jnp.float32)
    gate_sigmoid = jax.nn.sigmoid(gate_pre)
    active = gate_pre * gate_sigmoid
    hidden = (active * up_pre).astype(jnp.bfloat16)
    master = down_master[0]
    down_half = master.astype(jnp.bfloat16)
    grad_hidden = lax.dot_general(
        upstream,
        lax.all_gather(down_half, "dp", axis=1, tiled=True),
        (((1,), (1,)), ((), ())),
        preferred_element_type=jnp.float32,
    )
    grad_up = (grad_hidden * active).astype(jnp.bfloat16)
    grad_gate = (
        grad_hidden * up_pre * gate_sigmoid * (1.0 + gate_pre * (1.0 - gate_sigmoid))
    ).astype(jnp.bfloat16)
    first_part = lax.dot_general(
        grad_gate, gate_full, (((1,), (1,)), ((), ())), preferred_element_type=jnp.float32
    )
    second_part = lax.dot_general(
        grad_up, up_full, (((1,), (1,)), ((), ())), preferred_element_type=jnp.float32
    )
    input_grad = lax.psum_scatter(
        (first_part + second_part).astype(jnp.bfloat16), "mp", scatter_dimension=0, tiled=True
    )
    full_grad = lax.dot_general(
        hidden, upstream, (((0,), (0,)), ((), ())), preferred_element_type=jnp.float32
    )
    grad_down = lax.psum_scatter(
        full_grad.astype(jnp.bfloat16), "dp", scatter_dimension=1, tiled=True
    ).astype(jnp.float32)
    first_new = 0.9 * first_moment[0] + 0.1 * grad_down
    second_new = 0.999 * second_moment[0] + 0.001 * grad_down * grad_down
    adam_step = first_new / bias_one / (jnp.sqrt(second_new / bias_two) + 1e-08) + 0.1 * master
    inner_params = master - 0.001 * adam_step
    drift_local = anchor - inner_params
    mean_drift = lax.psum(drift_local.astype(jnp.bfloat16), "outer").astype(
        jnp.float32
    ) / lax.axis_size("outer")
    momentum_out = 0.9 * outer_momentum + mean_drift
    new_params = anchor - 0.7 * (mean_drift + 0.9 * momentum_out)
    return (new_params, first_new[None], second_new[None], momentum_out, input_grad[None])


def solution(mesh):
    return jax.shard_map(
        shards,
        mesh=mesh,
        in_specs=(
            P("outer", "dp", None),
            P("outer", "dp", None),
            P("outer", "dp", "mp"),
            P("outer", "dp", "mp"),
            P("outer", "mp", "dp"),
            P("outer", "mp", "dp"),
            P("outer", "mp", "dp"),
            P("mp", "dp"),
            P("mp", "dp"),
        ),
        out_specs=(
            P("mp", "dp"),
            P("outer", "mp", "dp"),
            P("outer", "mp", "dp"),
            P("mp", "dp"),
            P("outer", ("dp", "mp"), None),
        ),
        check_vma=False,
    )
```

profile of v0, /device:TPU:0, one launch (start us, length us, event | category | flops | bytes accessed | tf_op | source)
XLA Modules:
  0.0 1029.5 jit_solution(1354484625341851611)
XLA Ops:
  7.2 0.0 all-gather.8.cloned.1.call-start
  7.2 0.7 all-gather.8.cloned.1.call-update
  7.9 0.0 all-gather.10.cloned.1.call-start
  7.9 0.7 all-gather.10.cloned.1.call-update
  8.6 0.0 all-gather.6.cloned.1.call-start
  8.7 4.9 bitcast_convert_fusion
  13.5 0.0 all-gather.6.cloned.1.call-update
  13.6 0.0 reduce-scatter.3.cloned.1.call-start
  13.6 216.9 %all-gather.8.cloned.1.call-done = bf16[1,2048,3072]{2,1,0:T(8,128)(2,1)} async-done(((bf16[1,512,3072]{2,1,0:T(8,128)(2,1)}), bf16[1,2048,3072]{2,1,0:T(8,128)(2,1)}) %all-gather.8.cloned.1.call-update) | async-done | bytes 12582928 | tf_op jit(solution)/shard_map/all_gather | solution.py:24
  230.5 19.0 %fusion.6 = f32[1024,3072]{1,0:T(8,128)} fusion(bf16[1,2048,3072]{2,1,0:T(8,128)(2,1)} %all-gather.8.cloned.1.call-done, bf16[1,1024,2048]{2,1,0:T(8,128)(2,1)} %param.9), kind=kOutput, calls=%fused_computation.6 | convolution fusion | flops 12884901888 | bytes 29360128 | tf_op jit(solution)/shard_map/dot_general | solution.py:27
  249.5 199.0 %all-gather.10.cloned.1.call-done = bf16[1,2048,3072]{2,1,0:T(8,128)(2,1)} async-done(((bf16[1,512,3072]{2,1,0:T(8,128)(2,1)}), bf16[1,2048,3072]{2,1,0:T(8,128)(2,1)}) %all-gather.10.cloned.1.call-update) | async-done | bytes 12582928 | tf_op jit(solution)/shard_map/all_gather | solution.py:25
  448.5 18.9 %fusion.2 = f32[1024,3072]{1,0:T(8,128)} fusion(bf16[1,2048,3072]{2,1,0:T(8,128)(2,1)} %all-gather.10.cloned.1.call-done, bf16[1,1024,2048]{2,1,0:T(8,128)(2,1)} %param.9), kind=kOutput, calls=%fused_computation.2 | convolution fusion | flops 12884901888 | bytes 29360128 | tf_op jit(solution)/shard_map/dot_general | solution.py:28
  467.4 22.5 %convolution_convert_fusion = bf16[3072,2048]{1,0:T(8,128)(2,1)} fusion(f32[1024,3072]{1,0:T(8,128)} %fusion.2, bf16[1,1024,2048]{2,1,0:T(8,128)(2,1)} %param.10, f32[1024,3072]{1,0:T(8,128)} %fusion.6), kind=kOutput, calls=%fused_computation.13 | convolution fusion | flops 12910067712 | bytes 41943040 | tf_op jit(solution)/shard_map/dot_general | solution.py:53
  489.9 0.0 all-reduce.2.cloned.1.call-start
  490.0 177.1 %all-gather.6.cloned.1.call-done = bf16[3072,2048]{1,0:T(8,128)(2,1)} async-done(((bf16[3072,512]{1,0:T(8,128)(2,1)}), bf16[3072,2048]{1,0:T(8,128)(2,1)}) %all-gather.6.cloned.1.call-update) | async-done | bytes 12582928 | tf_op jit(solution)/shard_map/all_gather | solution.py:36
  667.1 19.1 %fusion.15 = f32[1024,3072]{1,0:T(8,128)} fusion(bf16[3072,2048]{1,0:T(8,128)(2,1)} %all-gather.6.cloned.1.call-done, bf16[1,1024,2048]{2,1,0:T(8,128)(2,1)} %param.10), kind=kOutput, calls=%fused_computation.29 | convolution fusion | flops 12884901888 | bytes 29360128 | tf_op jit(solution)/shard_map/dot_general | solution.py:34
  686.2 22.4 %fusion = f32[1024,2048]{1,0:T(8,128)} fusion(bf16[1,2048,3072]{2,1,0:T(8,128)(2,1)} %all-gather.10.cloned.1.call-done, f32[1024,3072]{1,0:T(8,128)} %fusion.15, f32[1024,3072]{1,0:T(8,128)} %fusion.6), kind=kOutput, calls=%fused_computation | convolution fusion | flops 12903776256 | bytes 46137344 | tf_op jit(solution)/shard_map/dot_general | solution.py:47
  708.6 170.8 %reduce-scatter.3.cloned.1.call-done = bf16[3072,512]{1,0:T(8,128)(2,1)} async-done(((bf16[3072,2048]{1,0:T(8,128)(2,1)}), bf16[3072,512]{1,0:T(8,128)(2,1)}) %reduce-scatter.3.cloned.1.call-update) | async-done | bytes 3145744 | tf_op jit(solution)/shard_map/reduce_scatter | solution.py:56
  879.4 16.4 %fusion.23 = (f32[1,3072,512]{2,1,0:T(8,128)}, bf16[3072,512]{1,0:T(8,128)(2,1)}, f32[1,3072,512]{2,1,0:T(8,128)}) fusion(bf16[3072,512]{1,0:T(8,128)(2,1)} %reduce-scatter.3.cloned.1.call-done, f32[1,3072,512]{2,1,0:T(8,128)} %param.15, f32[3072,512]{1,0:T(8,128)} %param.16, f32[1,3072,512]{2,1,0:T(8,128)} %param.14, f32[1,3072,512]{2,1,0:T(8,128)} %param.13), kind=kLoop, calls=%fused_computation.35 | loop fusion | flops 28311552 | bytes 44040192 | tf_op jit(solution)/shard_map/broadcast_in_dim | solution.py:69
  895.8 0.0 reduce-scatter.5.cloned.1.call-start
  895.9 30.8 %add_convert_fusion = bf16[1024,2048]{1,0:T(8,128)(2,1)} fusion(f32[1024,2048]{1,0:T(8,128)} %fusion, bf16[1,2048,3072]{2,1,0:T(8,128)(2,1)} %all-gather.8.cloned.1.call-done, f32[1024,3072]{1,0:T(8,128)} %fusion.6, f32[1024,3072]{1,0:T(8,128)} %fusion.15, f32[1024,3072]{1,0:T(8,128)} %fusion.2), kind=kOutput, calls=%fused_computation.15 | convolution fusion | flops 12920553472 | bytes 62914560 | tf_op jit(solution)/shard_map/dot_general | solution.py:44
  926.7 38.8 %all-reduce.2.cloned.1.call-done = bf16[3072,512]{1,0:T(8,128)(2,1)} async-done(((bf16[3072,512]{1,0:T(8,128)(2,1)}), bf16[3072,512]{1,0:T(8,128)(2,1)}) %all-reduce.2.cloned.1.call-update) | async-done | bytes 3145744 | tf_op jit(solution)/shard_map/psum | solution.py:64
  965.5 9.6 multiply_subtract_fusion
  975.0 47.6 %reduce-scatter.5.cloned.1.call-done = bf16[512,2048]{1,0:T(8,128)(2,1)} async-done(((bf16[1024,2048]{1,0:T(8,128)(2,1)}), bf16[512,2048]{1,0:T(8,128)(2,1)}) %reduce-scatter.5.cloned.1.call-update) | async-done | bytes 2097168 | tf_op jit(solution)/shard_map/reduce_scatter | solution.py:50
  (3 shorter events, 0.0 us)
Async XLA Ops:
  7.2 223.3 %all-gather.8.cloned.1.call-start = ((), (), s32[]{:S(2)}) async-start(), calls=%async_computation.6 | async-start | bytes 15728640 | tf_op jit(solution)/shard_map/all_gather | solution.py:24
  7.9 440.6 %all-gather.10.cloned.1.call-start = ((), (), s32[]{:S(2)}) async-start(), calls=%async_computation.7 | async-start | bytes 15728640 | tf_op jit(solution)/shard_map/all_gather | solution.py:25
  8.6 658.4 %all-gather.6.cloned.1.call-start = ((), (), s32[]{:S(2)}) async-start(), calls=%async_computation.4 | async-start | bytes 15728640 | tf_op jit(solution)/shard_map/all_gather | solution.py:36
  13.6 865.8 %reduce-scatter.3.cloned.1.call-start = ((), (), s32[]{:S(2)}) async-start(), calls=%async_computation.2 | async-start | bytes 15728640 | tf_op jit(solution)/shard_map/reduce_scatter | solution.py:56
  489.9 475.5 %all-reduce.2.cloned.1.call-start = ((), (), s32[]{:S(2)}) async-start(), calls=%async_computation.3 | async-start | bytes 6291456 | tf_op jit(solution)/shard_map/psum | solution.py:64
  895.8 126.8 %reduce-scatter.5.cloned.1.call-start = ((), (), s32[]{:S(2)}) async-start(), calls=%async_computation.5 | async-start | bytes 6291456 | tf_op jit(solution)/shard_map/reduce_scatter | solution.py:50
Sparse Core Ops, SparseCore 0:
  9.6 220.8 all-gather.7
  232.1 216.3 all-gather.9
  450.7 216.3 all-gather.5
  669.3 210.0 reduce-scatter.2
  895.9 69.4 all-reduce.1
  968.2 54.3 reduce-scatter.4
where the time goes:
time: 1030 us
  waiting for transfers between devices  852 us (83%)
  matrix products  133 us (13%)
  other arithmetic  30.8 us (3%)
  between operations  14.1 us (1%)
    all_gather x1, waiting for transfers between devices, shards(): lax.all_gather(gate_weight[0], 'dp', axis=0, tiled=True)  217 us
    all_gather x1, waiting for transfers between devices, shards(): lax.all_gather(up_weight[0], 'dp', axis=0, tiled=True)  199 us
    all_gather x1, waiting for transfers between devices, shards(): lax.all_gather(down_half, 'dp', axis=1, tiled=True)  177 us
    reduce_scatter x1, waiting for transfers between devices, shards(): lax.psum_scatter(full_grad.astype(jnp.bfloat16), 'dp', scatter_dimension=...  171 us
    reduce_scatter x1, waiting for transfers between devices, shards(): lax.psum_scatter((first_part + second_part).astype(jnp.bfloat16), 'mp', s...  47.6 us
    psum x1, waiting for transfers between devices, shards(): lax.psum(drift_local.astype(jnp.bfloat16), 'outer').astype(jnp.float32)  38.8 us
    dot_general x1, matrix products, shards(): lax.dot_general(grad_gate, gate_full, (((1,), (1,)), ((), ())), preferred...  30.8 us
    dot_general x1, matrix products, shards(): lax.dot_general(hidden, upstream, (((0,), (0,)), ((), ())), preferred_ele...  22.5 us
  transfers between devices with their start and end apart: 6, of which 6 were waited for; matrix products, arithmetic and copies ran while one was open for 14% of the time, Pallas kernels for 0%

commit v1 on v0

v1 whole, which is shorter than its diff:
```python
import jax
import jax.numpy as jnp
from jax import lax
from jax.sharding import PartitionSpec as P

bias_one = 1.0 - (0.9**50) ** 2
bias_two = 1.0 - (0.999**50) ** 2

chunks = 2
depth = 2


def swap(value, axis, bit):
    pairs = [(i, i ^ bit) for i in range(4)]
    return lax.ppermute(value, axis, pairs)


def cut(value, start, size, axis):
    return lax.dynamic_slice_in_dim(value, start, size, axis)


def reorder(value, me):
    width = value.shape[1] // 4
    return jnp.concatenate(
        [cut(value, (me ^ k) * width, width, 1) for k in range(4)], axis=1
    )


def dot(a, b, ca, cb):
    return lax.dot_general(a, b, (((ca,), (cb,)), ((), ())), preferred_element_type=jnp.float32)


def shards(
    tokens,
    cotangent,
    gate_weight,
    up_weight,
    down_master,
    first_moment,
    second_moment,
    anchor,
    outer_momentum,
):
    me = lax.axis_index("dp")
    parity = me % 2
    mp_size = lax.axis_size("mp")
    mine_mp = lax.axis_index("mp")
    half = gate_weight.shape[2] // 2
    part = half // chunks
    rows = tokens.shape[1]
    master = down_master[0]
    down_half = master.astype(jnp.bfloat16)

    queues = {"middle": [], "end": []}

    def send(value, bit, queue, after=()):
        done = queues[queue]
        before = tuple(done[-depth : len(done) - depth + 1]) if len(done) >= depth else ()
        before = before + tuple(after)
        if before:
            value = lax.optimization_barrier((value,) + before)[0]
        result = swap(value, "dp", bit)
        done.append(result)
        return result

    def share(block):
        piece = cut(block, mine_mp * (rows // mp_size), rows // mp_size, 0)
        other = lax.all_gather(send(piece, 1, "end"), "mp", axis=0, tiled=True)
        return reorder(jnp.concatenate([block, other], axis=0), me)

    def gather(shard, axis, c, after=()):
        keep = cut(shard, (2 * c + parity) * part, part, axis)
        away = cut(shard, (2 * c + 1 - parity) * part, part, axis)
        far = [send(keep, 2, "middle"), send(away, 3, "middle", after)]
        pieces = [keep, send(away, 1, "end")] + far
        return jnp.concatenate(pieces, axis=1 - axis)

    inputs = share(tokens[0])
    upstream = share(cotangent[0])
    downs = [gather(down_half, 0, c) for c in range(chunks)]
    grad_hiddens = [dot(upstream, down, 1, 1) for down in downs]

    def term_of(grad_hidden, active, slope, gate_full, up_full):
        grad_up = (grad_hidden * active).astype(jnp.bfloat16)
        grad_gate = (grad_hidden * slope).astype(jnp.bfloat16)
        return dot(grad_gate, gate_full, 1, 1) + dot(grad_up, up_full, 1, 1)

    grads = []
    width = tokens.shape[2] // 4
    even = parity == 0
    total = None
    arrived = None
    full_grad = None
    for c in range(chunks):
        gate_full = gather(gate_weight[0], 1, c, grad_hiddens if c == 1 else ())
        up_full = gather(up_weight[0], 1, c, () if c == 0 else (full_grad,))
        if c > 0:
            up_full, total = lax.optimization_barrier((up_full, total))
        gate_pre = dot(inputs, gate_full, 1, 0)
        up_pre = dot(inputs, up_full, 1, 0)
        gate_sigmoid = jax.nn.sigmoid(gate_pre)
        active = gate_pre * gate_sigmoid
        slope = up_pre * gate_sigmoid * (1.0 + gate_pre * (1.0 - gate_sigmoid))
        hidden = (active * up_pre).astype(jnp.bfloat16)
        full_grad = dot(hidden, upstream, 0, 0).astype(jnp.bfloat16)
        if c == 0:
            total = term_of(grad_hiddens[c], active, slope, gate_full, up_full)
            grads.append(full_grad)
        else:
            grads.append(full_grad)
            front = (grad_hiddens[c], active, slope, gate_full, up_full)

    for c in range(chunks):
        full_grad = grads[c]
        arrived = send(full_grad[:, 2 * width :], 2, "middle")
        if c == 0:
            grad_hidden = lax.optimization_barrier((front[0], arrived, grads[1]))[0]
            total = total + term_of(grad_hidden, *front[1:])
        summed = full_grad[:, : 2 * width].astype(jnp.float32) + arrived.astype(jnp.float32)
        came = swap(summed[:, width:].astype(jnp.bfloat16), "dp", 1).astype(jnp.float32)
        kept = summed[:, :width]
        grads[c] = jnp.concatenate(
            [jnp.where(even, kept, came), jnp.where(even, came, kept)], axis=0
        )

    partial = reorder(total.astype(jnp.bfloat16), me)
    split = partial.reshape(2, mp_size, rows // mp_size, partial.shape[1])
    own, other = split[0], split[1]
    other_sum = lax.psum_scatter(other, "mp", scatter_dimension=0, tiled=True)[0]
    other_back = swap(other_sum, "dp", 1)
    own_sum = lax.psum_scatter(own, "mp", scatter_dimension=0, tiled=True)[0]
    input_grad = (own_sum.astype(jnp.float32) + other_back.astype(jnp.float32)).astype(
        jnp.bfloat16
    )

    def adam(grad_down, low, high):
        first_new = 0.9 * first_moment[0, low:high] + 0.1 * grad_down
        second_new = 0.999 * second_moment[0, low:high] + 0.001 * grad_down * grad_down
        return first_new, second_new

    core = lax.axis_index("outer") % 2
    first_core = core == 0
    means = []
    for c in range(chunks):
        low, high = 2 * c * part, 2 * (c + 1) * part
        first_new, second_new = adam(grads[c], low, high)
        adam_step = (
            first_new / bias_one / (jnp.sqrt(second_new / bias_two) + 1e-08)
            + 0.1 * master[low:high]
        )
        inner_params = master[low:high] - 0.001 * adam_step
        drift = (anchor[low:high] - inner_params).astype(jnp.bfloat16)
        near = cut(drift, core * part, part, 0)
        pair = near.astype(jnp.float32) + swap(
            cut(drift, (1 - core) * part, part, 0), "outer", 1
        ).astype(jnp.float32)
        pair = pair.astype(jnp.bfloat16)
        quad = pair.astype(jnp.float32) + swap(pair, "outer", 2).astype(jnp.float32)
        quad = quad.astype(jnp.bfloat16)
        back = swap(quad, "outer", 1)
        means += [jnp.where(first_core, quad, back), jnp.where(first_core, back, quad)]

    first_new, second_new = adam(jnp.concatenate(grads, axis=0), 0, master.shape[0])
    mean_drift = jnp.concatenate(means, axis=0).astype(jnp.float32) / 4.0
    momentum_out = 0.9 * outer_momentum + mean_drift
    new_params = anchor - 0.7 * (mean_drift + 0.9 * momentum_out)
    return (new_params, first_new[None], second_new[None], momentum_out, input_grad[None])


def solution(mesh):
    return jax.shard_map(
        shards,
        mesh=mesh,
        in_specs=(
            P("outer", "dp", None),
            P("outer", "dp", None),
            P("outer", "dp", "mp"),
            P("outer", "dp", "mp"),
            P("outer", "mp", "dp"),
            P("outer", "mp", "dp"),
            P("outer", "mp", "dp"),
            P("mp", "dp"),
            P("mp", "dp"),
        ),
        out_specs=(
            P("mp", "dp"),
            P("outer", "mp", "dp"),
            P("outer", "mp", "dp"),
            P("mp", "dp"),
            P("outer", ("dp", "mp"), None),
        ),
        check_vma=False,
    )
```

time: 1030 us -> 846 us (0.82)
  waiting for transfers between devices: 852 us -> 420 us
  starting transfers between devices: 0.24 us -> 124 us
  other arithmetic: 30.8 us -> 84.4 us
  matrix products: 133 us -> 175 us
  local copies, waits for them, and re-layouts: 0 us -> 23.3 us
    all_gather x3 -> x2, waiting for transfers between devices: 593 us -> 0.01 us  [share(): other = lax.all_gather(send(piece, 1, 'end'), 'mp', axis=0, tiled=True)]
    ppermute x0 -> x31, waiting for transfers between devices: none -> 420 us  [swap(): return lax.ppermute(value, axis, pairs)]
    reduce_scatter x2, waiting for transfers between devices: 218 us -> 0.01 us  [the longest x1 0.01 us: shards(): lax.psum_scatter(other, 'mp', scatter_dimension=0, tiled=True)[0]]
    ppermute x0 -> x31, starting transfers between devices: none -> 124 us  [swap(): return lax.ppermute(value, axis, pairs)]
    dot_general x6 -> x12, matrix products: 133 us -> 175 us  [dot(): lax.dot_general(a, b, (((ca,), (cb,)), ((), ())), preferred_element_type=...]
    psum x1 -> x0, waiting for transfers between devices: 38.8 us -> none  [shards(): lax.psum(drift_local.astype(jnp.bfloat16), 'outer').astype(jnp.float32)]
    convert_element_type x0 -> x6, other arithmetic: none -> 37.6 us  [the longest x1 17 us: shards(): partial = reorder(total.astype(jnp.bfloat16), me)]
    add x0 -> x3, other arithmetic: none -> 14.4 us  [the longest x1 11.6 us: adam(): 0.999 * second_moment[0, low:high] + 0.001 * grad_down * grad_down]
  transfers between devices with their start and end apart: 6 -> 35, of which waited for: 6 -> 19; matrix products, arithmetic and copies ran while one was open for 14% -> 25% of each run, Pallas kernels for 0% -> 0%
where the time goes in v1:
time: 846 us; the launch traced here: 842 us
  waiting for transfers between devices  420 us (50%)
  matrix products  175 us (21%)
  starting transfers between devices  124 us (15%)
  other arithmetic  84.4 us (10%)
  local copies, waits for them, and re-layouts  23.3 us (3%)
  between operations  15.1 us (2%)
    ppermute x31, waiting for transfers between devices, swap(): return lax.ppermute(value, axis, pairs)  420 us
    dot_general x12, matrix products, dot(): lax.dot_general(a, b, (((ca,), (cb,)), ((), ())), preferred_element_type=...  175 us
    ppermute x31, starting transfers between devices, swap(): return lax.ppermute(value, axis, pairs)  124 us
    convert_element_type x1, other arithmetic, shards(): partial = reorder(total.astype(jnp.bfloat16), me)  17 us
  transfers between devices with their start and end apart: 35, of which 19 were waited for; matrix products, arithmetic and copies ran while one was open for 25% of the time, Pallas kernels for 0%

profile of v1, /device:TPU:0, one launch (start us, length us, event | category | flops | bytes accessed | tf_op | source)
XLA Modules:
  0.0 841.9 jit_solution(4508094171686528765)
XLA Ops:
  12.0 45.6 %collective-permute-done.9 = bf16[512,2048]{1,0:T(8,128)(2,1)S(1)} collective-permute-done((bf16[512,2048]{1,0:T(8,128)(2,1)S(1)}, bf16[512,2048]{1,0:T(8,128)(2,1)S(1)}, u32[]{:S(2)}, u32[]{:S(2)}) %collective-permute-start.9) | collective-permute-done | bytes 2097184 | tf_op jit(solution)/shard_map/ppermute | solution.py:15
  68.1 31.9 %collective-permute-done.3 = bf16[768,512]{1,0:T(8,128)(2,1)S(1)} collective-permute-done((bf16[768,512]{1,0:T(8,128)(2,1)S(1)}, bf16[768,512]{1,0:T(8,128)(2,1)S(1)}, u32[]{:S(2)}, u32[]{:S(2)}) %collective-permute-start.3) | collective-permute-done | bytes 786464 | tf_op jit(solution)/shard_map/ppermute | solution.py:15
  106.0 40.0 %collective-permute-done.4 = bf16[768,512]{1,0:T(8,128)(2,1)S(1)} collective-permute-done((bf16[768,512]{1,0:T(8,128)(2,1)S(1)}, bf16[768,512]{1,0:T(8,128)(2,1)S(1)}, u32[]{:S(2)}, u32[]{:S(2)}) %collective-permute-start.4) | collective-permute-done | bytes 786464 | tf_op jit(solution)/shard_map/ppermute | solution.py:15
  149.4 15.3 %collective-permute-done.6 = bf16[768,512]{1,0:T(8,128)(2,1)S(1)} collective-permute-done((bf16[768,512]{1,0:T(8,128)(2,1)S(1)}, bf16[768,512]{1,0:T(8,128)(2,1)S(1)}, u32[]{:S(2)}, u32[]{:S(2)}) %collective-permute-start.6) | collective-permute-done | bytes 786464 | tf_op jit(solution)/shard_map/ppermute | solution.py:15
  168.1 41.3 %collective-permute-start.1 = (bf16[768,512]{1,0:T(8,128)(2,1)}, bf16[768,512]{1,0:T(8,128)(2,1)S(1)}, u32[]{:S(2)}, u32[]{:S(2)}) collective-permute-start(bf16[768,512]{1,0:T(8,128)(2,1)} %copy-done.37), channel_id=1, source_target_pairs={{0,2},{2,0},{4,6},{6,4},{1,3},{3,1},{5,7},{7,5},{8,10},{10,8},{12,... | collective-permute-start | bytes 2359304 | tf_op jit(solution)/shard_map/ppermute | solution.py:15
  226.0 13.5 %collective-permute-done.1 = bf16[768,512]{1,0:T(8,128)(2,1)S(1)} collective-permute-done((bf16[768,512]{1,0:T(8,128)(2,1)}, bf16[768,512]{1,0:T(8,128)(2,1)S(1)}, u32[]{:S(2)}, u32[]{:S(2)}) %collective-permute-start.1) | collective-permute-done | bytes 786464 | tf_op jit(solution)/shard_map/ppermute | solution.py:15
  242.6 20.4 %collective-permute-done.10 = bf16[768,512]{1,0:T(8,128)(2,1)S(1)} collective-permute-done((bf16[768,512]{1,0:T(8,128)(2,1)}, bf16[768,512]{1,0:T(8,128)(2,1)S(1)}, u32[]{:S(2)}, u32[]{:S(2)}) %collective-permute-start.10) | collective-permute-done | bytes 786464 | tf_op jit(solution)/shard_map/ppermute | solution.py:15
  263.0 27.0 %collective-permute-done.12 = bf16[512,768]{1,0:T(8,128)(2,1)S(1)} collective-permute-done((bf16[512,768]{1,0:T(8,128)(2,1)S(1)}, bf16[512,768]{1,0:T(8,128)(2,1)S(1)}, u32[]{:S(2)}, u32[]{:S(2)}) %collective-permute-start.12) | collective-permute-done | bytes 786464 | tf_op jit(solution)/shard_map/ppermute | solution.py:15
  309.9 20.6 %collective-permute-done.11 = bf16[512,768]{1,0:T(8,128)(2,1)S(1)} collective-permute-done((bf16[512,768]{1,0:T(8,128)(2,1)}, bf16[512,768]{1,0:T(8,128)(2,1)S(1)}, u32[]{:S(2)}, u32[]{:S(2)}) %collective-permute-start.11) | collective-permute-done | bytes 786464 | tf_op jit(solution)/shard_map/ppermute | solution.py:15
  330.4 27.0 %collective-permute-done.14 = bf16[512,768]{1,0:T(8,128)(2,1)S(1)} collective-permute-done((bf16[512,768]{1,0:T(8,128)(2,1)}, bf16[512,768]{1,0:T(8,128)(2,1)S(1)}, u32[]{:S(2)}, u32[]{:S(2)}) %collective-permute-start.14) | collective-permute-done | bytes 786464 | tf_op jit(solution)/shard_map/ppermute | solution.py:15
  362.6 13.5 %fusion.27 = f32[2048,768]{1,0:T(8,128)} fusion(bf16[768,512]{1,0:T(8,128)(2,1)} %collective-permute-done.7, bf16[768,512]{1,0:T(8,128)(2,1)} %copy-done.44, bf16[768,512]{1,0:T(8,128)(2,1)} %copy-done.54, bf16[768,512]{1,0:T(8,128)(2,1)S(1)} %copy-done.34, bf16[2048,512]{1,0:T(8,128)(2,1)S(1)} %get-tuple-element.64, ...), kind=kOutput, calls=%fused_computation.70 | convolution fusion | flops 6488588288 | bytes 17825792 | tf_op jit(solution)/shard_map/dot_general | solution.py:30
  417.9 16.5 %convolution_convert_fusion.1 = bf16[768,2048]{1,0:T(8,128)(2,1)S(1)} fusion(f32[2048,768]{1,0:T(8,128)} %fusion.57, f32[2048,768]{1,0:T(8,128)} %fusion.58, bf16[2048,512]{1,0:T(8,128)(2,1)} %copy-done.20, bf16[2048,512]{1,0:T(8,128)(2,1)} %copy-done.19, bf16[2048,512]{1,0:T(8,128)(2,1)} %copy-done.18, bf16[2048,512]{1,0:T(8,128)(2,1)} %copy-done.17), kind=kOutput, calls=%fused_computation.43 | convolution fusion | flops 6487015424 | bytes 24117248 | tf_op jit(solution)/shard_map/dot_general | solution.py:30
  435.8 13.9 %fusion.16 = f32[2048,2048]{1,0:T(8,128)} fusion(f32[2048,768]{1,0:T(8,128)} %fusion.19, f32[2048,768]{1,0:T(8,128)} %fusion.58, bf16[512,768]{1,0:T(8,128)(2,1)} %collective-permute-done.13, bf16[512,768]{1,0:T(8,128)(2,1)} %copy-done.45, bf16[512,768]{1,0:T(8,128)(2,1)} %copy-done.52, bf16[512,768]{1,0:T(8,128)(2,1)} %copy-done.35), kind=kOutput, calls=%fused_computation.56 | convolution fusion | flops 6464471040 | bytes 32505856 | tf_op jit(solution)/shard_map/dot_general | solution.py:30
  449.8 22.3 %convolution_add_fusion = f32[2048,2048]{1,0:T(8,128)} fusion(f32[2048,2048]{1,0:T(8,128)} %fusion.16, f32[2048,768]{1,0:T(8,128)} %fusion.19, f32[2048,768]{1,0:T(8,128)} %fusion.58, f32[2048,768]{1,0:T(8,128)} %fusion.57, bf16[512,768]{1,0:T(8,128)(2,1)} %copy-done.47, bf16[512,768]{1,0:T(8,128)(2,1)} %collective-permute-done.5, ...), kind=kOutput, calls=%fused_computation.21 | convolution fusion | flops 6474956800 | bytes 55574528 | tf_op jit(solution)/shard_map/dot_general | solution.py:30
  501.1 17.2 %convolution_convert_fusion = bf16[768,2048]{1,0:T(8,128)(2,1)} fusion(f32[2048,768]{1,0:T(8,128)} %fusion.73, f32[2048,768]{1,0:T(8,128)} %fusion.56, bf16[2048,512]{1,0:T(8,128)(2,1)} %copy-done.20, bf16[2048,512]{1,0:T(8,128)(2,1)} %copy-done.19, bf16[2048,512]{1,0:T(8,128)(2,1)} %copy-done.18, bf16[2048,512]{1,0:T(8,128)(2,1)} %copy-done.17), kind=kOutput, calls=%fused_computation.42 | convolution fusion | flops 6487015424 | bytes 24117248 | tf_op jit(solution)/shard_map/dot_general | solution.py:30
  526.1 15.5 %fusion.18 = f32[2048,2048]{1,0:T(8,128)} fusion(bf16[2048,768]{1,0:T(8,128)(2,1)S(1)} %pad_maximum_fusion.8, f32[2048,768]{1,0:T(8,128)} %fusion.27, f32[2048,768]{1,0:T(8,128)} %fusion.56), kind=kOutput, calls=%fused_computation.58 | convolution fusion | flops 6451888128 | bytes 32505856 | tf_op jit(solution)/shard_map/dot_general | solution.py:30
  541.6 21.4 %fusion.17 = f32[2048,2048]{1,0:T(8,128)} fusion(f32[2048,768]{1,0:T(8,128)} %fusion.27, f32[2048,768]{1,0:T(8,128)} %fusion.56, f32[2048,768]{1,0:T(8,128)} %fusion.73, bf16[512,768]{1,0:T(8,128)(2,1)} %collective-permute-done.22, bf16[512,768]{1,0:T(8,128)(2,1)S(1)} %copy-done.42, bf16[512,768]{1,0:T(8,128)(2,1)} %collective-permute-done.21, ...), kind=kOutput, calls=%fused_computation.57 | convolution fusion | flops 6470762496 | bytes 38797312 | tf_op jit(solution)/shard_map/dot_general | solution.py:30
  563.0 17.0 %add_convert_fusion = bf16[2048,2048]{1,0:T(8,128)(2,1)S(1)} fusion(f32[2048,2048]{1,0:T(8,128)} %convolution_add_fusion, f32[2048,2048]{1,0:T(8,128)} %fusion.17, f32[2048,2048]{1,0:T(8,128)} %fusion.18), kind=kLoop, calls=%fused_computation | loop fusion | flops 12582912 | bytes 58720256 | tf_op jit(solution)/shard_map/convert_element_type | solution.py:126
  587.8 45.5 %collective-permute-start.25 = (bf16[768,1024]{1,0:T(8,128)(2,1)S(1)}, bf16[768,1024]{1,0:T(8,128)(2,1)S(1)}, u32[]{:S(2)}, u32[]{:S(2)}) collective-permute-start(bf16[768,1024]{1,0:T(8,128)(2,1)S(1)} %slice.91), channel_id=1, source_target_pairs={{0,4},{2,6},{4,0},{6,2},{1,5},{3,7},{5,1},{7,3},{8,12},{10,14},{12... | collective-permute-start | bytes 4718600 | tf_op jit(solution)/shard_map/ppermute | solution.py:15
  635.6 65.1 %collective-permute-done.25 = bf16[768,1024]{1,0:T(8,128)(2,1)S(1)} collective-permute-done((bf16[768,1024]{1,0:T(8,128)(2,1)S(1)}, bf16[768,1024]{1,0:T(8,128)(2,1)S(1)}, u32[]{:S(2)}, u32[]{:S(2)}) %collective-permute-start.25) | collective-permute-done | bytes 1572896 | tf_op jit(solution)/shard_map/ppermute | solution.py:15
  706.3 17.3 %collective-permute-done.26 = bf16[768,512]{1,0:T(8,128)(2,1)} collective-permute-done((bf16[768,512]{1,0:T(8,128)(2,1)}, bf16[768,512]{1,0:T(8,128)(2,1)}, u32[]{:S(2)}, u32[]{:S(2)}) %collective-permute-start.26) | collective-permute-done | bytes 786464 | tf_op jit(solution)/shard_map/ppermute | solution.py:15
  747.4 16.2 %collective-permute-done.19 = bf16[768,512]{1,0:T(8,128)(2,1)} collective-permute-done((bf16[768,512]{1,0:T(8,128)(2,1)}, bf16[768,512]{1,0:T(8,128)(2,1)}, u32[]{:S(2)}, u32[]{:S(2)}) %collective-permute-start.19) | collective-permute-done | bytes 786464 | tf_op jit(solution)/shard_map/ppermute | solution.py:15
  766.1 13.6 %collective-permute-done.28 = bf16[768,512]{1,0:T(8,128)(2,1)} collective-permute-done((bf16[768,512]{1,0:T(8,128)(2,1)}, bf16[768,512]{1,0:T(8,128)(2,1)}, u32[]{:S(2)}, u32[]{:S(2)}) %collective-permute-start.28) | collective-permute-done | bytes 786464 | tf_op jit(solution)/shard_map/ppermute | solution.py:15
  803.4 27.1 %collective-permute-done.30 = bf16[512,2048]{1,0:T(8,128)(2,1)} collective-permute-done((bf16[512,2048]{1,0:T(8,128)(2,1)}, bf16[512,2048]{1,0:T(8,128)(2,1)}, u32[]{:S(2)}, u32[]{:S(2)}) %collective-permute-start.30) | collective-permute-done | bytes 2097184 | tf_op jit(solution)/shard_map/ppermute | solution.py:15
  (220 shorter events, 221.9 us)
Async XLA Ops:
  7.2 350.3 %all-gather.5.cloned.1.call-start = ((), (), s32[]{:S(2)}) async-start(), calls=%async_computation.3 | async-start | bytes 6291456 | tf_op jit(solution)/shard_map/all_gather | solution.py:68
  9.0 48.7 %collective-permute-start.9 = (bf16[512,2048]{1,0:T(8,128)(2,1)S(1)}, bf16[512,2048]{1,0:T(8,128)(2,1)S(1)}, u32[]{:S(2)}, u32[]{:S(2)}) collective-permute-start(bf16[512,2048]{1,0:T(8,128)(2,1)S(1)} %dynamic-slice_bitcast_fusion), channel_id=1, source_target_pairs={{0,2},{2,0},{4,6},{6,4},{1,3},{3,1},{5,7},{7,5},{8,10},{10,8},{12,... | collective-permute-start | bytes 6291464 | tf_op jit(solution)/shard_map/ppermute | solution.py:15
  59.0 331.8 %all-gather.3.cloned.1.call-start = ((), (), s32[]{:S(2)}) async-start(), calls=%async_computation.2 | async-start | bytes 6291456 | tf_op jit(solution)/shard_map/all_gather | solution.py:68
  66.4 101.7 %collective-permute-start = (bf16[512,2048]{1,0:T(8,128)(2,1)S(1)}, bf16[512,2048]{1,0:T(8,128)(2,1)}, u32[]{:S(2)}, u32[]{:S(2)}) collective-permute-start(bf16[512,2048]{1,0:T(8,128)(2,1)S(1)} %dynamic-slice_bitcast_fusion.1), channel_id=1, source_target_pairs={{0,2},{2,0},{4,6},{6,4},{1,3},{3,1},{5,7},{7,5},{8,10},{10,8},{12,... | collective-permute-start | bytes 6291464 | tf_op jit(solution)/shard_map/ppermute | solution.py:15
  100.9 63.8 %collective-permute-start.6 = (bf16[768,512]{1,0:T(8,128)(2,1)S(1)}, bf16[768,512]{1,0:T(8,128)(2,1)S(1)}, u32[]{:S(2)}, u32[]{:S(2)}) collective-permute-start(bf16[768,512]{1,0:T(8,128)(2,1)S(1)} %get-tuple-element.26), channel_id=1, source_target_pairs={{0,6},{2,4},{4,2},{6,0},{1,7},{3,5},{5,3},{7,1},{8,14},{10,12},{12... | collective-permute-start | bytes 2359304 | tf_op jit(solution)/shard_map/ppermute | solution.py:15
  146.0 76.6 %collective-permute-start.5 = (bf16[512,768]{1,0:T(8,128)(2,1)}, bf16[512,768]{1,0:T(8,128)(2,1)}, u32[]{:S(2)}, u32[]{:S(2)}) collective-permute-start(bf16[512,768]{1,0:T(8,128)(2,1)} %get-tuple-element.29), channel_id=1, source_target_pairs={{0,4},{2,6},{4,0},{6,2},{1,5},{3,7},{5,1},{7,3},{8,12},{10,14},{12... | collective-permute-start | bytes 2359304 | tf_op jit(solution)/shard_map/ppermute | solution.py:15
  165.6 57.1 %collective-permute-start.7 = (bf16[768,512]{1,0:T(8,128)(2,1)}, bf16[768,512]{1,0:T(8,128)(2,1)}, u32[]{:S(2)}, u32[]{:S(2)}) collective-permute-start(bf16[768,512]{1,0:T(8,128)(2,1)} %get-tuple-element.32), channel_id=1, source_target_pairs={{0,6},{2,4},{4,2},{6,0},{1,7},{3,5},{5,3},{7,1},{8,14},{10,12},{12... | collective-permute-start | bytes 2359304 | tf_op jit(solution)/shard_map/ppermute | solution.py:15
  168.1 71.3 %collective-permute-start.1 = (bf16[768,512]{1,0:T(8,128)(2,1)}, bf16[768,512]{1,0:T(8,128)(2,1)S(1)}, u32[]{:S(2)}, u32[]{:S(2)}) collective-permute-start(bf16[768,512]{1,0:T(8,128)(2,1)} %copy-done.37), channel_id=1, source_target_pairs={{0,2},{2,0},{4,6},{6,4},{1,3},{3,1},{5,7},{7,5},{8,10},{10,8},{12,... | collective-permute-start | bytes 2359304 | tf_op jit(solution)/shard_map/ppermute | solution.py:15
  211.0 52.0 %collective-permute-start.10 = (bf16[768,512]{1,0:T(8,128)(2,1)}, bf16[768,512]{1,0:T(8,128)(2,1)S(1)}, u32[]{:S(2)}, u32[]{:S(2)}) collective-permute-start(bf16[768,512]{1,0:T(8,128)(2,1)} %get-tuple-element.32), channel_id=1, source_target_pairs={{0,2},{2,0},{4,6},{6,4},{1,3},{3,1},{5,7},{7,5},{8,10},{10,8},{12,... | collective-permute-start | bytes 2359304 | tf_op jit(solution)/shard_map/ppermute | solution.py:15
  222.7 67.3 %collective-permute-start.12 = (bf16[512,768]{1,0:T(8,128)(2,1)S(1)}, bf16[512,768]{1,0:T(8,128)(2,1)S(1)}, u32[]{:S(2)}, u32[]{:S(2)}) collective-permute-start(bf16[512,768]{1,0:T(8,128)(2,1)S(1)} %get-tuple-element.34), channel_id=1, source_target_pairs={{0,4},{2,6},{4,0},{6,2},{1,5},{3,7},{5,1},{7,3},{8,12},{10,14},{12... | collective-permute-start | bytes 2359304 | tf_op jit(solution)/shard_map/ppermute | solution.py:15
  222.7 68.4 %collective-permute-start.8 = (bf16[512,768]{1,0:T(8,128)(2,1)}, bf16[512,768]{1,0:T(8,128)(2,1)S(1)}, u32[]{:S(2)}, u32[]{:S(2)}) collective-permute-start(bf16[512,768]{1,0:T(8,128)(2,1)} %get-tuple-element.27), channel_id=1, source_target_pairs={{0,6},{2,4},{4,2},{6,0},{1,7},{3,5},{5,3},{7,1},{8,14},{10,12},{12... | collective-permute-start | bytes 2359304 | tf_op jit(solution)/shard_map/ppermute | solution.py:15
  239.5 67.4 %collective-permute-start.2 = (bf16[512,768]{1,0:T(8,128)(2,1)}, bf16[512,768]{1,0:T(8,128)(2,1)S(1)}, u32[]{:S(2)}, u32[]{:S(2)}) collective-permute-start(bf16[512,768]{1,0:T(8,128)(2,1)} %get-tuple-element.27), channel_id=1, source_target_pairs={{0,2},{2,0},{4,6},{6,4},{1,3},{3,1},{5,7},{7,5},{8,10},{10,8},{12,... | collective-permute-start | bytes 2359304 | tf_op jit(solution)/shard_map/ppermute | solution.py:15
  263.0 67.5 %collective-permute-start.11 = (bf16[512,768]{1,0:T(8,128)(2,1)}, bf16[512,768]{1,0:T(8,128)(2,1)S(1)}, u32[]{:S(2)}, u32[]{:S(2)}) collective-permute-start(bf16[512,768]{1,0:T(8,128)(2,1)} %get-tuple-element.33), channel_id=1, source_target_pairs={{0,2},{2,0},{4,6},{6,4},{1,3},{3,1},{5,7},{7,5},{8,10},{10,8},{12,... | collective-permute-start | bytes 2359304 | tf_op jit(solution)/shard_map/ppermute | solution.py:15
  291.0 66.5 %collective-permute-start.14 = (bf16[512,768]{1,0:T(8,128)(2,1)}, bf16[512,768]{1,0:T(8,128)(2,1)S(1)}, u32[]{:S(2)}, u32[]{:S(2)}) collective-permute-start(bf16[512,768]{1,0:T(8,128)(2,1)} %get-tuple-element.36), channel_id=1, source_target_pairs={{0,4},{2,6},{4,0},{6,2},{1,5},{3,7},{5,1},{7,3},{8,12},{10,14},{12... | collective-permute-start | bytes 2359304 | tf_op jit(solution)/shard_map/ppermute | solution.py:15
  291.0 491.2 %reduce-scatter.5.cloned.1.call-start = ((), (), s32[]{:S(2)}) async-start(), calls=%async_computation.5 | async-start | bytes 6291456 | tf_op jit(solution)/shard_map/reduce_scatter | solution.py:129
  291.1 96.5 %collective-permute-start.13 = (bf16[512,768]{1,0:T(8,128)(2,1)}, bf16[512,768]{1,0:T(8,128)(2,1)}, u32[]{:S(2)}, u32[]{:S(2)}) collective-permute-start(bf16[512,768]{1,0:T(8,128)(2,1)} %get-tuple-element.33), channel_id=1, source_target_pairs={{0,6},{2,4},{4,2},{6,0},{1,7},{3,5},{5,3},{7,1},{8,14},{10,12},{12... | collective-permute-start | bytes 2359304 | tf_op jit(solution)/shard_map/ppermute | solution.py:15
  306.9 166.3 %collective-permute-start.21 = (bf16[512,768]{1,0:T(8,128)(2,1)}, bf16[512,768]{1,0:T(8,128)(2,1)}, u32[]{:S(2)}, u32[]{:S(2)}) collective-permute-start(bf16[512,768]{1,0:T(8,128)(2,1)} %get-tuple-element.39), channel_id=1, source_target_pairs={{0,2},{2,0},{4,6},{6,4},{1,3},{3,1},{5,7},{7,5},{8,10},{10,8},{12,... | collective-permute-start | bytes 2359304 | tf_op jit(solution)/shard_map/ppermute | solution.py:15
  330.4 154.4 %collective-permute-start.23 = (bf16[512,768]{1,0:T(8,128)(2,1)}, bf16[512,768]{1,0:T(8,128)(2,1)}, u32[]{:S(2)}, u32[]{:S(2)}) collective-permute-start(bf16[512,768]{1,0:T(8,128)(2,1)} %get-tuple-element.41), channel_id=1, source_target_pairs={{0,2},{2,0},{4,6},{6,4},{1,3},{3,1},{5,7},{7,5},{8,10},{10,8},{12,... | collective-permute-start | bytes 2359304 | tf_op jit(solution)/shard_map/ppermute | solution.py:15
  357.5 77.1 %collective-permute-start.15 = (bf16[512,768]{1,0:T(8,128)(2,1)}, bf16[512,768]{1,0:T(8,128)(2,1)}, u32[]{:S(2)}, u32[]{:S(2)}) collective-permute-start(bf16[512,768]{1,0:T(8,128)(2,1)} %get-tuple-element.37), channel_id=1, source_target_pairs={{0,4},{2,6},{4,0},{6,2},{1,5},{3,7},{5,1},{7,3},{8,12},{10,14},{12... | collective-permute-start | bytes 2359304 | tf_op jit(solution)/shard_map/ppermute | solution.py:15
  387.6 84.5 %collective-permute-start.22 = (bf16[512,768]{1,0:T(8,128)(2,1)}, bf16[512,768]{1,0:T(8,128)(2,1)}, u32[]{:S(2)}, u32[]{:S(2)}) collective-permute-start(bf16[512,768]{1,0:T(8,128)(2,1)} %get-tuple-element.39), channel_id=1, source_target_pairs={{0,6},{2,4},{4,2},{6,0},{1,7},{3,5},{5,3},{7,1},{8,14},{10,12},{12... | collective-permute-start | bytes 2359304 | tf_op jit(solution)/shard_map/ppermute | solution.py:15
  434.6 91.5 %collective-permute-start.16 = (bf16[768,1024]{1,0:T(8,128)(2,1)S(1)}, bf16[768,1024]{1,0:T(8,128)(2,1)}, u32[]{:S(2)}, u32[]{:S(2)}) collective-permute-start(bf16[768,1024]{1,0:T(8,128)(2,1)S(1)} %slice.87), channel_id=1, source_target_pairs={{0,4},{2,6},{4,0},{6,2},{1,5},{3,7},{5,1},{7,3},{8,12},{10,14},{12... | collective-permute-start | bytes 4718600 | tf_op jit(solution)/shard_map/ppermute | solution.py:15
  586.0 217.4 %reduce-scatter.3.cloned.1.call-start = ((), (), s32[]{:S(2)}) async-start(), calls=%async_computation.4 | async-start | bytes 6291456 | tf_op jit(solution)/shard_map/reduce_scatter | solution.py:131
  587.8 112.9 %collective-permute-start.25 = (bf16[768,1024]{1,0:T(8,128)(2,1)S(1)}, bf16[768,1024]{1,0:T(8,128)(2,1)S(1)}, u32[]{:S(2)}, u32[]{:S(2)}) collective-permute-start(bf16[768,1024]{1,0:T(8,128)(2,1)S(1)} %slice.91), channel_id=1, source_target_pairs={{0,4},{2,6},{4,0},{6,2},{1,5},{3,7},{5,1},{7,3},{8,12},{10,14},{12... | collective-permute-start | bytes 4718600 | tf_op jit(solution)/shard_map/ppermute | solution.py:15
  635.5 68.6 %collective-permute-start.17 = (bf16[768,512]{1,0:T(8,128)(2,1)S(1)}, bf16[768,512]{1,0:T(8,128)(2,1)}, u32[]{:S(2)}, u32[]{:S(2)}) collective-permute-start(bf16[768,512]{1,0:T(8,128)(2,1)S(1)} %slice.113), channel_id=1, source_target_pairs={{0,2},{2,0},{4,6},{6,4},{1,3},{3,1},{5,7},{7,5},{8,10},{10,8},{12,... | collective-permute-start | bytes 2359304 | tf_op jit(solution)/shard_map/ppermute | solution.py:15
  (72 other events, 1680.4 us)
Sparse Core Ops, SparseCore 0:
  59.1 58.1 all-gather.4
  291.1 58.2 all-gather.2
  586.2 97.3 reduce-scatter.4
  704.2 53.9 reduce-scatter.2
